TPU v7x, 32 devices: a whole 2x2x4 slice. The times are simulated.
32 devices in a mesh: orb: 8 (over z, x), seg: 4 (over y, core).
Axes of the slice: x: 2, y: 2, z: 4, core: 2. Of those that a mesh axis runs over, the one named last changes fastest.
Arguments:
- coeffs: bfloat16 [64, 8192, 128], P('orb', 'seg'), as said below
- seg_count: int32 [4], P('seg'), may hold values from 1 to 2048, 4096 in all
- seg_lines: int32 [4, 2048], P('seg'), may hold values from 0 to 4095, as said below
- potential: float32 [128, 128, 128], P('seg'), may hold values from -1.5 to 0.5
Outputs:
- rotated_orbitals: bfloat16 [64, 8192, 128], P('orb', 'seg')
- rotated_applied: bfloat16 [64, 8192, 128], P('orb', 'seg')
- rotated_hamiltonian: float32 [64, 64], replicated
Inputs may be any that keep to these rules, and one draw needn't show every extreme that they name: `seg_count`: the counts of the 4 regions sum to 4096. `seg_lines`: within one region the entries are distinct. `coeffs`: only the live slots are read.
All inputs are finite; a program needn't handle non-finite values. No bound on the sum of `seg_count` on one device may be relied on, other than what follows from the above.
Results may differ from a plain program's by a relative error of at most 0.0013.
The roundings to bfloat16 on the way count: a program that leaves them out, or rounds other values in their place, can miss the bound.
Values may be sent and summed in bfloat16 or wider, within the bound.
No kernel may reach another device: no remote copies, remote signals or barrier semaphores. Data moves between devices by JAX's collectives and lax.ppermute only.
A program may use at most 128 MiB of HBM per device.

v0:
```python
import math

import jax
import jax.numpy as jnp
from jax import lax
from jax.sharding import PartitionSpec as P

SWEEPS = 6


RADIUS = 7
KINETIC = -0.5 / 2.25


def padded_2(cells, sides, width):
    for axis, dim in sides:
        count = lax.axis_size(axis)
        ends = count - 1
        head = lax.slice_in_dim(cells, 0, width, axis=dim)
        tail = lax.slice_in_dim(cells, cells.shape[dim] - width, cells.shape[dim], axis=dim)
        cells = jnp.concatenate(
            [
                lax.ppermute(tail, axis, [(i, (i + 1) % count) for i in range(ends)]),
                cells,
                lax.ppermute(head, axis, [((i + 1) % count, i) for i in range(ends)]),
            ],
            axis=dim,
        )
    return cells


def filter_taps():
    offsets = jnp.arange(-RADIUS, RADIUS + 1)
    safe_k = jnp.where(offsets == 0, 1, offsets).astype(jnp.float32)
    signs = jnp.where(offsets % 2 == 0, -1.0, 1.0).astype(jnp.float32)
    values = jnp.where(offsets == 0, -math.pi * math.pi / 3.0, 2.0 * signs / (safe_k * safe_k))
    return values.astype(jnp.bfloat16)


def band_table(n_in, n_out, shift):
    weights = filter_taps().astype(jnp.float32)
    offsets = jnp.arange(-RADIUS, RADIUS + 1)
    spread = jnp.arange(n_in)[:, None] - jnp.arange(n_out)[None, :] - shift
    table = jnp.sum(
        jnp.where(
            spread[:, :, None] == offsets[None, None, :],
            weights[None, None, :],
            jnp.zeros((), jnp.float32),
        ),
        axis=2,
    )
    return table.astype(jnp.bfloat16)


def inverse_root(intersection):
    high = lax.Precision.HIGHEST
    norm_scale = jnp.sqrt(jnp.sum(intersection * intersection) + 1e-06)
    identity = jnp.eye(intersection.shape[0], dtype=jnp.float32)
    upper = intersection / norm_scale
    lower = identity
    for sweep_id in range(SWEEPS):
        middle = 0.5 * (3.0 * identity - jnp.dot(lower, upper, precision=high))
        upper = jnp.dot(upper, middle, precision=high)
        lower = jnp.dot(middle, lower, precision=high)
    return lower / jnp.sqrt(norm_scale)


def body(coeffs, seg_count, seg_lines, potential):
    orbs, slot_count, depth = coeffs.shape
    cells_x, cells_y = (potential.shape[0], potential.shape[1])
    live_slots = jnp.arange(slot_count) < seg_count[0]
    line_index = seg_lines[0]
    kept_rows = jnp.where(live_slots[None, :, None], coeffs, jnp.zeros((), jnp.bfloat16))
    source_slot = (
        jnp.full((cells_x * cells_y,), slot_count, jnp.int32)
        .at[line_index]
        .set(jnp.arange(slot_count, dtype=jnp.int32))
    )
    extended = jnp.concatenate([kept_rows, jnp.zeros((orbs, 1, depth), jnp.bfloat16)], axis=1)
    grid_cells = jnp.take(extended, source_slot, axis=1)
    grid_cells = grid_cells.reshape(orbs, cells_x, cells_y, depth)
    padded = padded_2(grid_cells, (("seg", 1),), RADIUS)
    band_x = band_table(cells_x + 2 * RADIUS, cells_x, RADIUS)
    band_y = band_table(cells_y, cells_y, 0)
    band_z = band_table(depth, depth, 0)
    sweep_x = jnp.einsum("ba,obyz->oayz", band_x, padded, preferred_element_type=jnp.float32)
    sweep_y = jnp.einsum("obyz,yc->obcz", grid_cells, band_y, preferred_element_type=jnp.float32)
    sweep_z = jnp.einsum("obyz,zc->obyc", grid_cells, band_z, preferred_element_type=jnp.float32)
    applied = KINETIC * (sweep_x + sweep_y + sweep_z) + potential[None] * grid_cells.astype(
        jnp.float32
    )
    picked = applied.reshape(orbs, cells_x * cells_y, depth)[:, line_index]
    applied_rows = jnp.where(live_slots[None, :, None], picked, jnp.zeros((), jnp.float32)).astype(
        jnp.bfloat16
    )
    slot_orbitals, slot_applied = (
        lax.all_to_all(kept_rows, "orb", split_axis=1, concat_axis=0, tiled=True),
        lax.all_to_all(applied_rows, "orb", split_axis=1, concat_axis=0, tiled=True),
    )
    intersection_part = jnp.einsum(
        "osz,psz->op", slot_orbitals, slot_orbitals, preferred_element_type=jnp.float32
    )
    energy_part = jnp.einsum(
        "osz,psz->op", slot_orbitals, slot_applied, preferred_element_type=jnp.float32
    )
    intersection_sum, energy_sum = lax.psum((intersection_part, energy_part), ("orb", "seg"))
    weight_sum = 2.0 / (lax.axis_size("seg") * slot_count * depth)
    intersection = intersection_sum * weight_sum
    hamiltonian = energy_sum * weight_sum
    rotation = inverse_root(intersection)
    rotation_half = rotation.astype(jnp.bfloat16)
    turned_orbitals = jnp.einsum(
        "op,osz->psz", rotation_half, slot_orbitals, preferred_element_type=jnp.float32
    ).astype(jnp.bfloat16)
    turned_applied = jnp.einsum(
        "op,osz->psz", rotation_half, slot_applied, preferred_element_type=jnp.float32
    ).astype(jnp.bfloat16)
    rotated_orbitals, rotated_applied = (
        lax.all_to_all(turned_orbitals, "orb", split_axis=0, concat_axis=1, tiled=True),
        lax.all_to_all(turned_applied, "orb", split_axis=0, concat_axis=1, tiled=True),
    )
    high = lax.Precision.HIGHEST
    rotated_hamiltonian = jnp.dot(
        jnp.dot(rotation.T, hamiltonian, precision=high), rotation, precision=high
    )
    return (rotated_orbitals, rotated_applied, rotated_hamiltonian)


def solution(mesh):
    in_specs = (P("orb", "seg", None), P("seg"), P("seg", None), P("seg", None, None))
    out_specs = (P("orb", "seg", None), P("orb", "seg", None), P())
    return jax.shard_map(body, mesh=mesh, in_specs=in_specs, out_specs=out_specs, check_vma=False)
```

profile of v0, /device:TPU:0, one launch (start us, length us, event | category | flops | bytes accessed | tf_op | source)
XLA Modules:
  0.0 548.2 jit_solution(17106958611994993847)
XLA Ops:
  1.3 15.0 %copy_select_fusion.1 = bf16[8,2048,128]{2,0,1:T(8,128)(2,1)} fusion(bf16[8,2048,128]{2,1,0:T(8,128)(2,1)} %param.4, pred[2048]{0:T(1024)(128)(4,1)S(1)} %iota_compare_fusion.3), kind=kLoop, calls=%fused_computation.27 | loop fusion | flops 2097152 | bytes 8390656 | tf_op jit(solution)/shard_map/jit(_where)/select_n | solution.py:73
  16.3 7.4 %all-to-all-start = ((bf16[8,2048,128]{2,0,1:T(8,128)(2,1)}), bf16[8,2048,128]{2,0,1:T(8,128)(2,1)}, u32[]{:S(2)}, u32[]{:S(2)}) async-start(bf16[8,2048,128]{2,0,1:T(8,128)(2,1)} %copy_select_fusion.1), calls=%async_computation | async-start | bytes 8388608 | tf_op jit(solution)/shard_map/all_to_all | solution.py:97
  23.7 8.1 %scatter_custom_fusion = s32[4096]{0:T(1024)S(1)} fusion(s32[2048]{0:T(1024)S(1)} %bitcast.120, s32[2048]{0:T(1024)S(1)} %iota.95, s32[]{:T(128)} %constant.34.clone.1), kind=kCustom, calls=%fused_computation.75 | custom fusion | bytes 16388 | tf_op jit(solution)/shard_map/scatter | solution.py:77
  31.8 5.1 concatenate.6
  36.9 0.1 copy.67
  37.0 31.2 %gather_fusion = bf16[4096,8,128]{2,1,0:T(8,128)(2,1)} fusion(bf16[8,2049,128]{2,0,1:T(8,128)(2,1)} %concatenate.6, s32[4096]{0:T(1024)S(1)} %fusion.59), kind=kCustom, calls=%fused_computation | custom fusion | bytes 16793600 | tf_op jit(solution)/shard_map/jit(_take)/gather | solution.py:80
  68.2 17.8 %copy_select_fusion = bf16[8,32,128,128]{3,1,2,0:T(8,128)(2,1)S(1)} fusion(bf16[8,32,128,128]{3,0,2,1:T(8,128)(2,1)} %bitcast.116, pred[32,128]{0,1:T(8,128)(4,1)S(1)} %copy.67), kind=kLoop, calls=%fused_computation.13 | loop fusion | flops 4194304 | bytes 16781312 | tf_op jit(solution)/shard_map/jit(_take)/select_n | solution.py:80
  86.0 0.9 fusion.78
  86.9 0.0 copy-start
  86.9 0.5 copy.70
  87.5 1.7 collective-permute-start
  89.2 0.5 copy.71
  89.7 1.5 collective-permute-start.1
  91.2 0.0 copy-done
  91.2 1.2 copy.79
  92.5 0.2 select_reduce_fusion
  92.7 0.1 select_reduce_fusion.1
  92.8 9.0 %fusion.11 = f32[128,8,32,128]{3,0,2,1:T(8,128)} fusion(bf16[8,32,128,128]{3,1,2,0:T(8,128)(2,1)S(1)} %copy_select_fusion, bf16[128,128]{1,0:T(8,128)(2,1)S(1)} %select_reduce_fusion), kind=kOutput, calls=%fused_computation.14 | convolution fusion | flops 1073741824 | bytes 25198592 | tf_op jit(solution)/shard_map/obyz,yc->obcz/dot_general | solution.py:87
  101.8 7.1 %fusion.48 = f32[8,32,128,128]{3,1,2,0:T(8,128)} fusion(bf16[8,32,128,128]{3,1,2,0:T(8,128)(2,1)S(1)} %copy_select_fusion, bf16[128,128]{1,0:T(8,128)(2,1)S(1)} %select_reduce_fusion), kind=kOutput, calls=%fused_computation.55 | convolution fusion | flops 1073741824 | bytes 25198592 | tf_op jit(solution)/shard_map/obyz,zc->obyc/dot_general | solution.py:88
  109.0 0.0 collective-permute-done
  109.0 1.2 copy.72
  110.2 0.0 collective-permute-done.1
  110.2 2.5 copy.73
  112.8 21.5 %fusion.2 = bf16[8,32,128,128]{3,1,2,0:T(8,128)(2,1)} fusion(f32[8,32,128,128]{3,1,2,0:T(8,128)} %fusion.48, f32[128,8,32,128]{3,0,2,1:T(8,128)} %fusion.11, bf16[8,32,128,128]{3,1,2,0:T(8,128)(2,1)S(1)} %copy_select_fusion, bf16[8,7,128,128]{3,1,2,0:T(8,128)(2,1)} %copy.73, bf16[8,7,128,128]{3,1,2,0:T(8,128)(2,1)S(1)} %copy.72, ...), kind=kOutput, calls=%fused_computation.6 | convolution fusion | flops 451411968 | bytes 56101760 | tf_op jit(solution)/shard_map/ba,obyz->oayz/dot_general | solution.py:86
  134.2 9.8 %copy.80 = bf16[8,32,128,128]{3,2,1,0:T(8,128)(2,1)} copy(bf16[8,32,128,128]{3,1,2,0:T(8,128)(2,1)} %fusion.2) | data formatting | bytes 16777216 | tf_op jit(solution)/shard_map/add | solution.py:89
  144.1 18.2 %copy.81 = bf16[8,4096,128]{2,0,1:T(8,128)(2,1)} copy(bf16[8,4096,128]{2,1,0:T(8,128)(2,1)} %bitcast.117) | data formatting | bytes 16777216 | tf_op jit(solution)/shard_map/reshape | solution.py:92
  162.3 18.0 %gather_fusion.1 = bf16[2048,8,128]{2,1,0:T(8,128)(2,1)} fusion(bf16[8,4096,128]{2,0,1:T(8,128)(2,1)} %copy.81, s32[2048]{0:T(1024)S(1)} %broadcast_clamp_fusion), kind=kCustom, calls=%fused_computation.1 | custom fusion | bytes 8396800 | tf_op jit(solution)/shard_map/gather | solution.py:92
  180.3 10.9 %fusion.13 = bf16[8,2048,128]{2,0,1:T(8,128)(2,1)} fusion(bf16[2048,8,128]{2,1,0:T(8,128)(2,1)} %gather_fusion.1, pred[2048]{0:T(1024)(128)(4,1)S(1)} %iota_compare_fusion.3), kind=kLoop, calls=%fused_computation.17 | loop fusion | flops 2097152 | bytes 8390656 | tf_op jit(solution)/shard_map/convert_element_type | solution.py:93
  191.2 0.0 all-to-all-done
  191.2 5.8 %all-to-all-start.2 = ((bf16[8,2048,128]{2,0,1:T(8,128)(2,1)}), bf16[8,2048,128]{2,0,1:T(8,128)(2,1)}, u32[]{:S(2)}, u32[]{:S(2)}) async-start(bf16[8,2048,128]{2,0,1:T(8,128)(2,1)} %fusion.13), calls=%async_computation.2 | async-start | bytes 8388608 | tf_op jit(solution)/shard_map/all_to_all | solution.py:98
  197.0 4.7 fusion.34
  201.7 85.5 %all-to-all-done.2 = bf16[8,2048,128]{2,0,1:T(8,128)(2,1)} async-done(((bf16[8,2048,128]{2,0,1:T(8,128)(2,1)}), bf16[8,2048,128]{2,0,1:T(8,128)(2,1)}, u32[]{:S(2)}, u32[]{:S(2)}) %all-to-all-start.2) | async-done | bytes 4194336 | tf_op jit(solution)/shard_map/all_to_all | solution.py:98
  287.2 4.7 fusion.37
  291.9 43.4 %all-reduce.1 = (f32[64,64]{1,0:T(8,128)S(1)}, f32[64,64]{1,0:T(8,128)S(1)}) all-reduce(f32[64,64]{1,0:T(8,128)S(1)} %fusion.34, f32[64,64]{1,0:T(8,128)S(1)} %fusion.37), channel_id=1, replica_groups=mesh['orb'=8,'seg'=4] {'orb','seg'}, use_global_device_ids=true, to_apply=%region_0.1 | all-reduce | flops 8192 | bytes 65536 | tf_op jit(solution)/shard_map/psum | solution.py:106
  335.3 0.6 multiply_reduce_fusion
  336.6 0.2 fusion.47
  336.7 0.2 fusion.60
  336.9 0.1 fusion.53
  337.1 0.2 fusion.46
  337.2 0.2 fusion.80
  337.4 0.2 fusion.79
  337.6 0.2 fusion.45
  337.7 0.2 fusion.82
  337.9 0.2 fusion.81
  338.1 0.2 fusion.44
  338.3 0.2 fusion.84
  338.4 0.2 fusion.83
  338.6 0.2 fusion.43
  338.8 0.2 fusion.86
  338.9 0.2 fusion.85
  339.1 0.2 fusion.42
  339.3 0.2 convolution_divide_fusion
  339.5 3.5 fusion.28
  343.0 4.7 copy.85
  347.7 6.2 %all-to-all-start.3 = ((bf16[64,256,128]{2,1,0:T(8,128)(2,1)}), bf16[64,256,128]{2,1,0:T(8,128)(2,1)}, u32[]{:S(2)}, u32[]{:S(2)}) async-start(bf16[64,256,128]{2,1,0:T(8,128)(2,1)} %copy.85), calls=%async_computation.3 | async-start | bytes 8388608 | tf_op jit(solution)/shard_map/all_to_all | solution.py:120
  353.9 3.5 fusion.31
  357.3 4.7 copy.65
  362.0 84.1 %all-to-all-done.3 = bf16[64,256,128]{2,1,0:T(8,128)(2,1)} async-done(((bf16[64,256,128]{2,1,0:T(8,128)(2,1)}), bf16[64,256,128]{2,1,0:T(8,128)(2,1)}, u32[]{:S(2)}, u32[]{:S(2)}) %all-to-all-start.3) | async-done | bytes 4194336 | tf_op jit(solution)/shard_map/all_to_all | solution.py:120
  446.2 4.5 all-to-all-start.1
  450.7 0.2 fusion.51
  451.0 0.8 fusion.87
  451.7 4.7 copy.86
  456.4 86.9 %all-to-all-done.1 = bf16[64,256,128]{2,1,0:T(8,128)(2,1)} async-done(((bf16[64,256,128]{2,1,0:T(8,128)(2,1)}), bf16[64,256,128]{2,1,0:T(8,128)(2,1)}, u32[]{:S(2)}, u32[]{:S(2)}) %all-to-all-start.1) | async-done | bytes 4194336 | tf_op jit(solution)/shard_map/all_to_all | solution.py:119
  543.3 4.7 copy.66
  (12 shorter events, 0.1 us)
Async XLA Ops:
  16.3 7.4 %copy-start.1 = (s32[1,2048]{1,0:T(1,128)S(1)}, s32[1,2048]{1,0:T(1,128)}, u32[]{:S(2)}) copy-start(s32[1,2048]{1,0:T(1,128)} %param.6) | copy-start | bytes 24580
  16.3 174.9 %all-to-all-start = ((bf16[8,2048,128]{2,0,1:T(8,128)(2,1)}), bf16[8,2048,128]{2,0,1:T(8,128)(2,1)}, u32[]{:S(2)}, u32[]{:S(2)}) async-start(bf16[8,2048,128]{2,0,1:T(8,128)(2,1)} %copy_select_fusion.1), calls=%async_computation | async-start | bytes 8388608 | tf_op jit(solution)/shard_map/all_to_all | solution.py:97
  86.9 4.3 copy-start
  87.5 21.5 %collective-permute-start = (bf16[8,7,128,128]{3,2,1,0:T(8,128)(2,1)S(1)}, bf16[8,7,128,128]{3,2,1,0:T(8,128)(2,1)S(1)}, u32[]{:S(2)}, u32[]{:S(2)}) collective-permute-start(bf16[8,7,128,128]{3,2,1,0:T(8,128)(2,1)S(1)} %copy.70), channel_id=1, source_target_pairs={{0,1},{1,2},{2,3},{4,5},{5,6},{6,7},{8,9},{9,10},{10,11},{12,13},{... | collective-permute-start | bytes 5505032 | tf_op jit(solution)/shard_map/ppermute | solution.py:23
  89.7 20.5 %collective-permute-start.1 = (bf16[8,7,128,128]{3,2,1,0:T(8,128)(2,1)S(1)}, bf16[8,7,128,128]{3,2,1,0:T(8,128)(2,1)S(1)}, u32[]{:S(2)}, u32[]{:S(2)}) collective-permute-start(bf16[8,7,128,128]{3,2,1,0:T(8,128)(2,1)S(1)} %copy.71), channel_id=1, source_target_pairs={{1,0},{2,1},{3,2},{5,4},{6,5},{7,6},{9,8},{10,9},{11,10},{13,12},{... | collective-permute-start | bytes 5505032 | tf_op jit(solution)/shard_map/ppermute | solution.py:25
  191.2 96.0 %all-to-all-start.2 = ((bf16[8,2048,128]{2,0,1:T(8,128)(2,1)}), bf16[8,2048,128]{2,0,1:T(8,128)(2,1)}, u32[]{:S(2)}, u32[]{:S(2)}) async-start(bf16[8,2048,128]{2,0,1:T(8,128)(2,1)} %fusion.13), calls=%async_computation.2 | async-start | bytes 8388608 | tf_op jit(solution)/shard_map/all_to_all | solution.py:98
  347.7 98.5 %all-to-all-start.3 = ((bf16[64,256,128]{2,1,0:T(8,128)(2,1)}), bf16[64,256,128]{2,1,0:T(8,128)(2,1)}, u32[]{:S(2)}, u32[]{:S(2)}) async-start(bf16[64,256,128]{2,1,0:T(8,128)(2,1)} %copy.85), calls=%async_computation.3 | async-start | bytes 8388608 | tf_op jit(solution)/shard_map/all_to_all | solution.py:120
  446.2 97.1 %all-to-all-start.1 = ((bf16[64,256,128]{2,1,0:T(8,128)(2,1)}), bf16[64,256,128]{2,1,0:T(8,128)(2,1)}, u32[]{:S(2)}, u32[]{:S(2)}) async-start(bf16[64,256,128]{2,1,0:T(8,128)(2,1)} %copy.65), calls=%async_computation.1 | async-start | bytes 8388608 | tf_op jit(solution)/shard_map/all_to_all | solution.py:119
where the time goes:
time: 552 us; the launch traced here: 548 us
  waiting for transfers between devices  256 us (46%)
  local copies, waits for them, and re-layouts  116 us (21%)
  matrix products  57.7 us (10%)
  other arithmetic  44.6 us (8%)
  blocking collectives  43.4 us (8%)
  starting transfers between devices  27.2 us (5%)
    all_to_all x1, waiting for transfers between devices, body(): lax.all_to_all(turned_orbitals, 'orb', split_axis=0, concat_axis=1, tiled...  86.9 us
    all_to_all x1, waiting for transfers between devices, body(): lax.all_to_all(applied_rows, 'orb', split_axis=1, concat_axis=0, tiled=True)  85.5 us
    all_to_all x1, waiting for transfers between devices, body(): lax.all_to_all(turned_applied, 'orb', split_axis=0, concat_axis=1, tiled=...  84.1 us
    psum x1, blocking collectives, body(): lax.psum((intersection_part, energy_part), ('orb', 'seg'))  43.4 us
    gather x1, local copies, waits for them, and re-layouts, body(): grid_cells = jnp.take(extended, source_slot, axis=1)  31.2 us
    dot_general x1, matrix products, body(): jnp.einsum('ba,obyz->oayz', band_x, padded, preferred_element_type=jnp.fl...  21.5 us
    reshape x1, local copies, waits for them, and re-layouts, body(): picked = applied.reshape(orbs, cells_x * cells_y, depth)[:, line_index]  18.2 us
    gather x1, local copies, waits for them, and re-layouts, body(): picked = applied.reshape(orbs, cells_x * cells_y, depth)[:, line_index]  18 us
  transfers between devices with their start and end apart: 6, of which 3 were waited for; matrix products, arithmetic and copies ran while one was open for 33% of the time, Pallas kernels for 0%

commit v1 on v0

v1 whole, which is shorter than its diff:
```python
import functools
import math

import jax
import jax.numpy as jnp
import ml_dtypes
import numpy as np
from jax import lax
from jax.experimental import pallas as pl
from jax.experimental.pallas import tpu as pltpu
from jax.sharding import PartitionSpec as P

SWEEPS = 6
RADIUS = 7
KINETIC = -0.5 / 2.25
TILE = 256
GROUP = 8
PITCH_PAD = 16
VMEM = 60 * 1024 * 1024


def tap_values():
    exact = [-math.pi * math.pi / 3.0]
    exact += [2.0 * (1.0 if k % 2 else -1.0) / (k * k) for k in range(1, RADIUS + 1)]
    return [float(np.float32(v).astype(ml_dtypes.bfloat16)) for v in exact]


TAPS = tap_values()


def band_matrix(n):
    table = np.zeros((n, n), np.float32)
    for i in range(n):
        for j in range(n):
            if abs(i - j) <= RADIUS:
                table[i, j] = TAPS[abs(i - j)]
    return table.astype(ml_dtypes.bfloat16)


def inverse_root(intersection):
    high = lax.Precision.HIGHEST
    norm_scale = jnp.sqrt(jnp.sum(intersection * intersection) + 1e-06)
    identity = jnp.eye(intersection.shape[0], dtype=jnp.float32)
    upper = intersection / norm_scale
    lower = identity
    for sweep_id in range(SWEEPS):
        middle = 0.5 * (3.0 * identity - jnp.dot(lower, upper, precision=high))
        upper = jnp.dot(upper, middle, precision=high)
        lower = jnp.dot(middle, lower, precision=high)
    return lower / jnp.sqrt(norm_scale)


def swapped(value, axis, distance):
    size = lax.axis_size(axis)
    return lax.ppermute(value, axis, [(i, i ^ distance) for i in range(size)])


def bits(axis):
    size = lax.axis_size(axis)
    return [1 << b for b in range(size.bit_length() - 1)]


def total(value):
    for axis in ("seg", "orb"):
        for distance in bits(axis):
            value = value + swapped(value, axis, distance)
    return value


def pack_kernel(edge_lines, grid_lines, count_ref, lines_ref, coeffs_ref, rows_ref, edge_ref):
    step = pl.program_id(0)
    count = count_ref[0]
    base = step * TILE
    live = count - base
    dump = 2 * edge_lines

    @pl.when(step == 0)
    def _():
        edge_ref[...] = jnp.zeros_like(edge_ref)

    @pl.when(live > 0)
    def _():
        tile = jnp.swapaxes(coeffs_ref[...].astype(jnp.float32), 0, 1)
        row = lax.broadcasted_iota(jnp.int32, tile.shape, 0)
        rows_ref[...] = jnp.where(row < live, tile, 0.0).astype(jnp.bfloat16)

        @pl.loop(0, TILE // GROUP)
        def _(group):
            for u in range(GROUP):
                j = group * GROUP + u
                line = lines_ref[base + j]
                tail = line - (grid_lines - 2 * edge_lines)
                place = jnp.where(line < edge_lines, line, jnp.where(tail >= edge_lines, tail, dump))
                place = jnp.where(j < live, place, dump)
                edge_ref[place] = rows_ref[j]

    @pl.when(live <= 0)
    def _():
        rows_ref[...] = jnp.zeros_like(rows_ref)


def pack(coeffs, seg_count, lines, grid_lines, cells_y, rows_out):
    orbs, slot_count, depth = coeffs.shape
    edge_lines = RADIUS * cells_y
    last = slot_count // TILE - 1
    return pl.pallas_call(
        functools.partial(pack_kernel, edge_lines, grid_lines),
        grid=(rows_out // TILE,),
        in_specs=[
            pl.BlockSpec(memory_space=pltpu.SMEM),
            pl.BlockSpec(memory_space=pltpu.SMEM),
            pl.BlockSpec((orbs, TILE, depth), lambda i: (0, jnp.minimum(i, last), 0)),
        ],
        out_specs=[
            pl.BlockSpec((TILE, orbs, depth), lambda i: (i, 0, 0)),
            pl.BlockSpec((2 * edge_lines + 8, orbs, depth), lambda i: (0, 0, 0)),
        ],
        out_shape=[
            jax.ShapeDtypeStruct((rows_out, orbs, depth), jnp.bfloat16),
            jax.ShapeDtypeStruct((2 * edge_lines + 8, orbs, depth), jnp.bfloat16),
        ],
        compiler_params=pltpu.CompilerParams(vmem_limit_bytes=VMEM),
        cost_estimate=pl.CostEstimate(flops=0, bytes_accessed=14 << 20, transcendentals=0),
        name="pack_slots",
    )(seg_count, lines, coeffs)


def apply_kernel(
    cells_x,
    cells_y,
    count_ref,
    lines_ref,
    rows_ref,
    low_ref,
    high_ref,
    potential_ref,
    band_ref,
    applied_ref,
    grid_ref,
    zsum_ref,
):
    step = pl.program_id(0)
    pitch = cells_y + PITCH_PAD
    count = count_ref[0]
    base = step * TILE
    live = jnp.minimum(count - base, TILE)
    shift = cells_y.bit_length() - 1

    def place_of(line):
        return line + lax.shift_right_logical(line, shift) * PITCH_PAD + (RADIUS * pitch + RADIUS)

    @pl.when(step == 0)
    def _():
        @pl.loop(0, grid_ref.shape[0] // 16)
        def _(block):
            grid_ref[pl.ds(block * 16, 16)] = jnp.zeros((16,) + grid_ref.shape[1:], jnp.float32)

        for plane in range(RADIUS):
            for source, at in ((low_ref, plane), (high_ref, plane + RADIUS + cells_x)):

                @pl.loop(0, cells_y // 16)
                def _(block, source=source, at=at, plane=plane):
                    grid_ref[pl.ds(at * pitch + RADIUS + block * 16, 16)] = source[
                        pl.ds(plane * cells_y + block * 16, 16)
                    ].astype(jnp.float32)

        @pl.loop(0, lax.div(count + GROUP - 1, GROUP))
        def _(group):
            for u in range(GROUP):
                j = group * GROUP + u
                place = jnp.where(j < count, place_of(lines_ref[j]), grid_ref.shape[0] - 1)
                grid_ref[place] = rows_ref[j].astype(jnp.float32)

    applied_ref[...] = jnp.zeros_like(applied_ref)

    @pl.when(live > 0)
    def _():
        tile = rows_ref[pl.ds(base, TILE)].astype(jnp.float32)
        flat = tile.reshape(TILE * tile.shape[1], tile.shape[2]).astype(jnp.bfloat16)
        zsum = jnp.dot(flat, band_ref[...], preferred_element_type=jnp.float32)
        zsum_ref[...] = (KINETIC * zsum).reshape(zsum_ref.shape)

        @pl.loop(0, lax.div(live + GROUP - 1, GROUP))
        def _(group):
            for u in range(GROUP):
                j = group * GROUP + u
                line = lines_ref[base + j]
                at = place_of(line)
                center = grid_ref[at]
                value = zsum_ref[j] + center * (
                    potential_ref[pl.ds(line, 1), :] + (2.0 * KINETIC * TAPS[0])
                )
                for k in range(1, RADIUS + 1):
                    near = (grid_ref[at - k] + grid_ref[at + k]) + (
                        grid_ref[at - k * pitch] + grid_ref[at + k * pitch]
                    )
                    value = value + (KINETIC * TAPS[k]) * near
                applied_ref[j] = jnp.where(j < live, value, 0.0).astype(jnp.bfloat16)


def apply_rows(rows, seg_count, lines, low, high, potential):
    rows_out, orbs, depth = rows.shape
    cells_x, cells_y, _ = potential.shape
    slot_count = lines.shape[0]
    edge_lines = RADIUS * cells_y
    pitch = cells_y + PITCH_PAD
    grid_rows = (cells_x + 2 * RADIUS) * pitch + 16
    once = pl.Buffered(1)
    whole = lambda i: (0, 0, 0)
    return pl.pallas_call(
        functools.partial(apply_kernel, cells_x, cells_y),
        grid=(rows_out // TILE,),
        in_specs=[
            pl.BlockSpec(memory_space=pltpu.SMEM),
            pl.BlockSpec(memory_space=pltpu.SMEM),
            pl.BlockSpec((slot_count, orbs, depth), whole, pipeline_mode=once),
            pl.BlockSpec((edge_lines, orbs, depth), whole, pipeline_mode=once),
            pl.BlockSpec((edge_lines, orbs, depth), whole, pipeline_mode=once),
            pl.BlockSpec((cells_x * cells_y, depth), lambda i: (0, 0), pipeline_mode=once),
            pl.BlockSpec((depth, depth), lambda i: (0, 0), pipeline_mode=once),
        ],
        out_specs=pl.BlockSpec((TILE, orbs, depth), lambda i: (i, 0, 0)),
        out_shape=jax.ShapeDtypeStruct((rows_out, orbs, depth), jnp.bfloat16),
        scratch_shapes=[
            pltpu.VMEM((grid_rows, orbs, depth), jnp.float32),
            pltpu.VMEM((TILE, orbs, depth), jnp.float32),
        ],
        compiler_params=pltpu.CompilerParams(vmem_limit_bytes=VMEM),
        cost_estimate=pl.CostEstimate(flops=2 << 30, bytes_accessed=60 << 20, transcendentals=0),
        name="apply_rows",
    )(
        seg_count,
        lines,
        rows,
        low,
        high,
        potential.reshape(cells_x * cells_y, depth),
        jnp.asarray(band_matrix(depth)),
    )


def unpack_kernel(rows_ref, out_ref):
    tile = jnp.swapaxes(rows_ref[...].astype(jnp.float32), 0, 1)
    out_ref[...] = tile.astype(jnp.bfloat16)


def unpack(rows, slot_count):
    _, orbs, depth = rows.shape
    return pl.pallas_call(
        unpack_kernel,
        grid=(slot_count // TILE,),
        in_specs=[pl.BlockSpec((TILE, orbs, depth), lambda i: (i, 0, 0))],
        out_specs=pl.BlockSpec((orbs, TILE, depth), lambda i: (0, i, 0)),
        out_shape=jax.ShapeDtypeStruct((orbs, slot_count, depth), jnp.bfloat16),
        compiler_params=pltpu.CompilerParams(vmem_limit_bytes=VMEM),
        cost_estimate=pl.CostEstimate(flops=0, bytes_accessed=8 << 20, transcendentals=0),
        name="unpack_slots",
    )(rows)


def body(coeffs, seg_count, seg_lines, potential):
    orbs, slot_count, depth = coeffs.shape
    cells_x, cells_y, _ = potential.shape
    n_orb, n_seg = lax.axis_size("orb"), lax.axis_size("seg")
    lines = seg_lines[0]
    move = slot_count // 2
    padded = slot_count + move
    edge_lines = RADIUS * cells_y
    weight_sum = 2.0 / (n_seg * slot_count * depth)

    partner_count = swapped(seg_count, "seg", 1)
    both = seg_count + partner_count
    core = lax.rem(lax.axis_index("seg"), 2)
    share = (both[0] + 1 - core) // 2
    own = jnp.minimum(seg_count[0], share)
    most = (both + 1) // 2
    for distance in bits("seg")[1:]:
        most = jnp.maximum(most, swapped(most, "seg", distance))

    rows, edges = pack(coeffs, seg_count, lines, cells_x * cells_y, cells_y, padded)

    def balance(value, start):
        sent = lax.dynamic_slice_in_dim(value, start, move, axis=0)
        return lax.dynamic_update_slice_in_dim(value, swapped(sent, "seg", 1), own, axis=0)

    def rest(used, operands):
        rows, edges = operands
        part = used // n_orb
        ends = n_seg - 1

        def spread(value):
            return lax.all_to_all(value[:used], "orb", split_axis=0, concat_axis=0, tiled=True).reshape(
                n_orb, part, orbs, depth
            )

        def collect(value):
            value = lax.all_to_all(
                value.reshape(n_orb * part, orbs, depth), "orb", split_axis=0, concat_axis=0, tiled=True
            )
            value = jnp.pad(value, ((0, padded - used), (0, 0), (0, 0)))
            return unpack(balance(value, own), slot_count)

        slot_orbitals = spread(balance(rows, share))
        low = lax.ppermute(
            edges[edge_lines : 2 * edge_lines], "seg", [(i, i + 1) for i in range(ends)]
        )
        high = lax.ppermute(edges[:edge_lines], "seg", [(i + 1, i) for i in range(ends)])
        applied = apply_rows(rows, seg_count, lines, low, high, potential)
        slot_applied = spread(balance(applied, share))

        def gram(left, right):
            return jnp.einsum("asoz,bspz->aobp", left, right, preferred_element_type=jnp.float32).reshape(
                n_orb * orbs, n_orb * orbs
            )

        intersection = total(gram(slot_orbitals, slot_orbitals)) * weight_sum
        rotation = inverse_root(intersection)
        half = rotation.astype(jnp.bfloat16).reshape(n_orb, orbs, n_orb, orbs)

        def turn(value):
            return jnp.einsum("aobp,asoz->bspz", half, value, preferred_element_type=jnp.float32).astype(
                jnp.bfloat16
            )

        rotated_orbitals = collect(turn(slot_orbitals))
        rotated_applied = collect(turn(slot_applied))
        hamiltonian = total(gram(slot_orbitals, slot_applied)) * weight_sum
        high_p = lax.Precision.HIGHEST
        rotated_hamiltonian = jnp.dot(
            jnp.dot(rotation.T, hamiltonian, precision=high_p), rotation, precision=high_p
        )
        return rotated_orbitals, rotated_applied, rotated_hamiltonian

    first = slot_count // 2
    grain = slot_count // 8
    classes = [first + grain * (i + 1) for i in range(4)]
    chosen = jnp.clip((most[0] - first + grain - 1) // grain - 1, 0, len(classes) - 1)
    return lax.switch(chosen, [functools.partial(rest, used) for used in classes], (rows, edges))


def solution(mesh):
    in_specs = (P("orb", "seg", None), P("seg"), P("seg", None), P("seg", None, None))
    out_specs = (P("orb", "seg", None), P("orb", "seg", None), P())
    return jax.shard_map(body, mesh=mesh, in_specs=in_specs, out_specs=out_specs, check_vma=False)
```

time: 552 us -> 451 us (0.82)
  starting transfers between devices: 27.2 us -> 120 us
  local copies, waits for them, and re-layouts: 116 us -> 56.1 us
  waiting for transfers between devices: 256 us -> 197 us
  Pallas kernels: 0 us -> 47.3 us
  matrix products: 57.7 us -> 11.9 us
  other arithmetic: 44.6 us -> 0.65 us
  blocking collectives: 43.4 us -> 0 us
  loops' own time: 0 us -> 13.1 us
    all_to_all x4, waiting for transfers between devices: 256 us -> 162 us  [the longest x2 131 us: collect(): lax.all_to_all(value.reshape(n_orb * part, orbs, depth), 'orb', split_axi...]
    ppermute x2 -> x18, starting transfers between devices: 3.25 us -> 96.3 us  [the longest x16 91.4 us: swapped(): return lax.ppermute(value, axis, [(i, i ^ distance) for i in range(size)])]
    gather x2 -> x0, local copies, waits for them, and re-layouts: 49.2 us -> none  [the longest x1 31.2 us: body(): grid_cells = jnp.take(extended, source_slot, axis=1)]
    pallas_call x0 -> x4, Pallas kernels: none -> 47.3 us  [the longest x1 20.2 us: apply_rows(): pl.pallas_call(functools.partial(apply_kernel, cells_x, cells_y), grid=(r...]
    dot_general x9 -> x6, matrix products: 55 us -> 9.12 us  [the longest x2 4.14 us: gram(): jnp.einsum('asoz,bspz->aobp', left, right, preferred_element_type=jnp.flo...]
    psum x1 -> x0, blocking collectives: 43.4 us -> none  [body(): lax.psum((intersection_part, energy_part), ('orb', 'seg'))]
    ppermute x2 -> x18, waiting for transfers between devices: 0.01 us -> 35.1 us  [the longest x16 31.1 us: swapped(): return lax.ppermute(value, axis, [(i, i ^ distance) for i in range(size)])]
    select_n x3 -> x0, other arithmetic: 32.8 us -> none  [the longest x1 17.8 us: body(): grid_cells = jnp.take(extended, source_slot, axis=1)]
  transfers between devices with their start and end apart: 6 -> 22, of which waited for: 3 -> 17; matrix products, arithmetic and copies ran while one was open for 33% -> 12% of each run, Pallas kernels for 0% -> 9%
where the time goes in v1:
time: 451 us; the launch traced here: 450 us
  waiting for transfers between devices  197 us (44%)
  starting transfers between devices  120 us (27%)
  local copies, waits for them, and re-layouts  56.1 us (12%)
  Pallas kernels  47.3 us (10%)
  loops' own time  13.1 us (3%)
  matrix products  11.9 us (3%)
    all_to_all x2, waiting for transfers between devices, collect(): lax.all_to_all(value.reshape(n_orb * part, orbs, depth), 'orb', split_axi...  131 us
    ppermute x16, starting transfers between devices, swapped(): return lax.ppermute(value, axis, [(i, i ^ distance) for i in range(size)])  91.4 us
    all_to_all x2, waiting for transfers between devices, spread(): lax.all_to_all(value[:used], 'orb', split_axis=0, concat_axis=0, tiled=True)  31.3 us
    ppermute x16, waiting for transfers between devices, swapped(): return lax.ppermute(value, axis, [(i, i ^ distance) for i in range(size)])  31.1 us
    pallas_call x1, Pallas kernels, apply_rows(): pl.pallas_call(functools.partial(apply_kernel, cells_x, cells_y), grid=(r...  20.2 us
    pad x2, local copies, waits for them, and re-layouts, collect(): value = jnp.pad(value, ((0, padded - used), (0, 0), (0, 0)))  18.4 us
    pallas_call x2, Pallas kernels, unpack(): pl.pallas_call(unpack_kernel, grid=(slot_count // TILE,), in_specs=[pl.Bl...  14.9 us
    dynamic_slice x4, local copies, waits for them, and re-layouts, balance(): sent = lax.dynamic_slice_in_dim(value, start, move, axis=0)  13.8 us
  transfers between devices with their start and end apart: 22, of which 17 were waited for; matrix products, arithmetic and copies ran while one was open for 12% of the time, Pallas kernels for 9%

profile of v1, /device:TPU:0, one launch (start us, length us, event | category | flops | bytes accessed | tf_op | source)
XLA Modules:
  0.0 449.8 jit_solution(8053694299268811829)
XLA Ops:
  0.7 0.5 collective-permute-start.64
  1.9 12.2 %pack_slots.1 = (bf16[3072,8,128]{2,1,0:T(8,128)(2,1)}, bf16[1800,8,128]{2,1,0:T(8,128)(2,1)}) custom-call(s32[1]{0:T(128)S(6)} %copy.251.count_ref, s32[2048]{0:T(1024)} %bitcast.361, bf16[8,2048,128]{2,1,0:T(8,128)(2,1)} %coeffs_ref.1), custom_call_target="tpu_custom_call" | custom-call | bytes 14680064 | tf_op jit(solution)/shard_map/pack_slots/pallas_call | solution.py:106
  14.8 7.5 %collective-permute-start.65 = (s32[1]{0:T(128)}, s32[1]{0:T(128)}, u32[]{:S(2)}, u32[]{:S(2)}) collective-permute-start(s32[1]{0:T(128)} %select_n.53), channel_id=1, source_target_pairs={{0,2},{1,3},{2,0},{3,1},{4,6},{5,7},{6,4},{7,5},{8,10},{9,11},{10,... | collective-permute-start | bytes 20 | tf_op jit(solution)/shard_map/ppermute | solution.py:55
  22.2 0.3 collective-permute-done.65
  23.2 425.2 %conditional.1 = (bf16[8,2048,128]{2,1,0:T(8,128)(2,1)}, bf16[8,2048,128]{2,1,0:T(8,128)(2,1)}, f32[64,64]{1,0:T(8,128)}) conditional(s32[]{:T(128)} %clamp.3, (s32[]{:T(128)}, bf16[3072,8,128]{2,1,0:T(8,128)(2,1)}, s32[1]{0:T(128)}, bf16[1800,8,128]{2,1,0:T(8,128)(2,1)}, f32[32,128,128]{2,1,0:T(8,128)S(1)}, ...), branch_computations={%region_0.2_spmd, %region_2.4_spmd, %region_4.6_spmd, %region_6.8_... | conditional | flops 3285385216 | bytes 324101088 | solution.py:338
  29.3 3.2 constant_dynamic-slice_fusion.3
  32.5 2.2 fusion.166
  34.6 3.7 collective-permute-start.23
  38.3 1.3 collective-permute-start.24
  40.2 0.5 collective-permute-done.23.low_ref
  40.8 3.5 collective-permute-done.24.high_ref
  44.3 20.2 %apply_rows.5 = bf16[3072,8,128]{2,1,0:T(8,128)(2,1)} custom-call(s32[1]{0:T(128)} %get-tuple-element.75.count_ref, s32[2048]{0:T(1024)S(1)} %get-tuple-element.76.lines_ref, bf16[3072,8,128]{2,1,0:T(8,128)(2,1)} %get-tuple-element.72.rows_ref, bf16[896,8,128]{2,1,0:T(8,128)(2,1)} %collective-permute-done.23.low_ref, ...), custom_call_target="tpu_custom_call" | custom-call | flops 2147483648 | bytes 62914560 | tf_op jit(solution)/shard_map/cond/branch_1_fun/apply_rows/pallas_call | solution.py:210
  64.5 3.1 constant_dynamic-update-slice_fusion.7
  67.6 3.2 slice.50
  70.8 5.8 %all-to-all-start.4 = ((bf16[1536,8,128]{2,1,0:T(8,128)(2,1)}), bf16[1536,8,128]{2,1,0:T(8,128)(2,1)S(1)}, u32[]{:S(2)}, u32[]{:S(2)}) async-start(bf16[1536,8,128]{2,1,0:T(8,128)(2,1)} %slice.50), calls=%async_computation.4 | async-start | bytes 6291456 | tf_op jit(solution)/shard_map/cond/branch_1_fun/all_to_all | solution.py:292
  76.6 1.7 constant_dynamic-slice_fusion.2
  78.3 21.7 %collective-permute-start.25 = (bf16[1024,8,128]{2,1,0:T(8,128)(2,1)S(1)}, bf16[1024,8,128]{2,1,0:T(8,128)(2,1)S(1)}, u32[]{:S(2)}, u32[]{:S(2)}) collective-permute-start(bf16[1024,8,128]{2,1,0:T(8,128)(2,1)S(1)} %constant_dynamic-slice_fusion.2), channel_id=1, source_target_pairs={{0,1},{1,0},{2,3},{3,2},{4,5},{5,4},{6,7},{7,6},{8,9},{9,8},{10,11... | collective-permute-start | bytes 6291464 | tf_op jit(solution)/shard_map/cond/branch_1_fun/ppermute | solution.py:55
  100.0 3.8 collective-permute-done.25
  103.7 1.5 constant_dynamic-update-slice_fusion.5
  105.2 3.2 slice.51
  108.4 31.3 %all-to-all-done.4 = bf16[1536,8,128]{2,1,0:T(8,128)(2,1)S(1)} async-done(((bf16[1536,8,128]{2,1,0:T(8,128)(2,1)}), bf16[1536,8,128]{2,1,0:T(8,128)(2,1)S(1)}, u32[]{:S(2)}, u32[]{:S(2)}) %all-to-all-start.4) | async-done | bytes 3145760 | tf_op jit(solution)/shard_map/cond/branch_1_fun/all_to_all | solution.py:292
  139.7 4.6 %all-to-all-start.6 = ((bf16[1536,8,128]{2,1,0:T(8,128)(2,1)}), bf16[1536,8,128]{2,1,0:T(8,128)(2,1)}, u32[]{:S(2)}, u32[]{:S(2)}) async-start(bf16[1536,8,128]{2,1,0:T(8,128)(2,1)} %slice.51), calls=%async_computation.6 | async-start | bytes 6291456 | tf_op jit(solution)/shard_map/cond/branch_1_fun/all_to_all | solution.py:292
  144.3 1.0 fusion.59
  145.3 13.1 %collective-permute-start.17 = (f32[64,64]{1,0:T(8,128)S(1)}, f32[64,64]{1,0:T(8,128)S(1)}, u32[]{:S(2)}, u32[]{:S(2)}) collective-permute-start(f32[64,64]{1,0:T(8,128)S(1)} %fusion.59), channel_id=1, source_target_pairs={{0,1},{1,0},{2,3},{3,2},{4,5},{5,4},{6,7},{7,6},{8,9},{9,8},{10,11... | collective-permute-start | bytes 49160 | tf_op jit(solution)/shard_map/cond/branch_1_fun/ppermute | solution.py:55
  158.4 0.9 collective-permute-done.17
  159.3 32.8 %collective-permute-start.18 = (f32[64,64]{1,0:T(8,128)S(1)}, f32[64,64]{1,0:T(8,128)S(1)}, u32[]{:S(2)}, u32[]{:S(2)}) collective-permute-start(f32[64,64]{1,0:T(8,128)S(1)} %add.170), channel_id=1, source_target_pairs={{0,2},{1,3},{2,0},{3,1},{4,6},{5,7},{6,4},{7,5},{8,10},{9,11},{10,... | collective-permute-start | bytes 49160 | tf_op jit(solution)/shard_map/cond/branch_1_fun/ppermute | solution.py:55
  192.1 1.9 collective-permute-done.18
  194.0 2.0 collective-permute-start.19
  196.0 2.1 collective-permute-done.19
  198.1 1.9 collective-permute-start.20
  199.9 2.4 collective-permute-done.20
  202.3 2.4 collective-permute-start.21
  204.8 6.8 %collective-permute-done.21 = f32[64,64]{1,0:T(8,128)S(1)} collective-permute-done((f32[64,64]{1,0:T(8,128)S(1)}, f32[64,64]{1,0:T(8,128)S(1)}, u32[]{:S(2)}, u32[]{:S(2)}) %collective-permute-start.21) | collective-permute-done | bytes 16416 | tf_op jit(solution)/shard_map/cond/branch_1_fun/ppermute | solution.py:55
  211.6 0.6 multiply_reduce_fusion.1
  213.3 0.2 fusion.80
  216.1 1.3 fusion.41
  217.4 2.2 copy.66
  219.7 6.2 %all-to-all-start.5 = ((bf16[1536,8,128]{2,1,0:T(8,128)(2,1)}), bf16[1536,8,128]{2,1,0:T(8,128)(2,1)S(1)}, u32[]{:S(2)}, u32[]{:S(2)}) async-start(bf16[1536,8,128]{2,1,0:T(8,128)(2,1)} %bitcast.352), calls=%async_computation.5 | async-start | bytes 6291456 | tf_op jit(solution)/shard_map/cond/branch_1_fun/all_to_all | solution.py:297
  225.8 2.7 fusion.42
  228.6 2.2 copy.69
  230.8 64.3 %all-to-all-done.5 = bf16[1536,8,128]{2,1,0:T(8,128)(2,1)S(1)} async-done(((bf16[1536,8,128]{2,1,0:T(8,128)(2,1)}), bf16[1536,8,128]{2,1,0:T(8,128)(2,1)S(1)}, u32[]{:S(2)}, u32[]{:S(2)}) %all-to-all-start.5) | async-done | bytes 3145760 | tf_op jit(solution)/shard_map/cond/branch_1_fun/all_to_all | solution.py:297
  295.1 6.7 %all-to-all-start.7 = ((bf16[1536,8,128]{2,1,0:T(8,128)(2,1)}), bf16[1536,8,128]{2,1,0:T(8,128)(2,1)}, u32[]{:S(2)}, u32[]{:S(2)}) async-start(bf16[1536,8,128]{2,1,0:T(8,128)(2,1)} %bitcast.351), calls=%async_computation.7 | async-start | bytes 6291456 | tf_op jit(solution)/shard_map/cond/branch_1_fun/all_to_all | solution.py:297
  301.8 5.1 %pad_dynamic-slice_fusion.3 = bf16[1024,8,128]{2,1,0:T(8,128)(2,1)} fusion(s32[]{:T(128)S(6)} %select_n.37, bf16[1536,8,128]{2,1,0:T(8,128)(2,1)S(1)} %all-to-all-done.5), kind=kLoop, calls=%fused_computation.84 | loop fusion | bytes 5242884 | tf_op jit(solution)/shard_map/cond/branch_1_fun/dynamic_slice | solution.py:283
  306.9 1.1 collective-permute-start.22
  308.0 66.3 %all-to-all-done.7 = bf16[1536,8,128]{2,1,0:T(8,128)(2,1)} async-done(((bf16[1536,8,128]{2,1,0:T(8,128)(2,1)}), bf16[1536,8,128]{2,1,0:T(8,128)(2,1)}, u32[]{:S(2)}, u32[]{:S(2)}) %all-to-all-start.7) | async-done | bytes 3145760 | tf_op jit(solution)/shard_map/cond/branch_1_fun/all_to_all | solution.py:297
  374.3 3.7 pad_dynamic-slice_fusion.2
  378.1 3.2 fusion.62
  381.3 0.5 collective-permute-start.27
  381.8 0.9 collective-permute-done.27
  382.7 5.3 %collective-permute-start.28 = (f32[64,64]{1,0:T(8,128)S(1)}, f32[64,64]{1,0:T(8,128)S(1)}, u32[]{:S(2)}, u32[]{:S(2)}) collective-permute-start(f32[64,64]{1,0:T(8,128)S(1)} %add.176), channel_id=1, source_target_pairs={{0,2},{1,3},{2,0},{3,1},{4,6},{5,7},{6,4},{7,5},{8,10},{9,11},{10,... | collective-permute-start | bytes 49160 | tf_op jit(solution)/shard_map/cond/branch_1_fun/ppermute | solution.py:55
  388.0 1.9 collective-permute-done.28
  389.9 1.5 collective-permute-start.29
  391.3 2.5 collective-permute-done.29
  393.8 3.9 collective-permute-done.30
  397.7 1.1 collective-permute-start.31
  398.8 3.8 collective-permute-done.31
  402.5 0.2 fusion.75
  402.8 0.8 fusion.189
  403.6 12.7 %pad.22 = bf16[3072,8,128]{2,1,0:T(8,128)(2,1)} pad(bf16[1536,8,128]{2,1,0:T(8,128)(2,1)S(1)} %all-to-all-done.5, bf16[]{:T(256)} %constant.105.clone), padding=0_1536x0_0x0_0 | pad | bytes 9437186 | tf_op jit(solution)/shard_map/cond/branch_1_fun/jit(_pad)/pad | solution.py:300
  416.2 5.7 %pad.23 = bf16[3072,8,128]{2,1,0:T(8,128)(2,1)} pad(bf16[1536,8,128]{2,1,0:T(8,128)(2,1)} %all-to-all-done.7, bf16[]{:T(256)} %constant.105.clone), padding=0_1536x0_0x0_0 | pad | bytes 9437186 | tf_op jit(solution)/shard_map/cond/branch_1_fun/jit(_pad)/pad | solution.py:300
  421.9 3.0 constant_dynamic-update-slice_fusion.6.rows_ref
  425.0 7.4 %unpack_slots.10 = bf16[8,2048,128]{2,1,0:T(8,128)(2,1)} custom-call(bf16[3072,8,128]{2,1,0:T(8,128)(2,1)} %constant_dynamic-update-slice_fusion.6.rows_ref), custom_call_target="tpu_custom_call" | custom-call | bytes 8388608 | tf_op jit(solution)/shard_map/cond/branch_1_fun/unpack_slots/pallas_call | solution.py:249
  432.4 3.1 constant_dynamic-update-slice_fusion.4.rows_ref
  435.5 7.4 %unpack_slots.11 = bf16[8,2048,128]{2,1,0:T(8,128)(2,1)} custom-call(bf16[3072,8,128]{2,1,0:T(8,128)(2,1)} %constant_dynamic-update-slice_fusion.4.rows_ref), custom_call_target="tpu_custom_call" | custom-call | bytes 8388608 | tf_op jit(solution)/shard_map/cond/branch_1_fun/unpack_slots/pallas_call | solution.py:249
  (44 shorter events, 3.0 us)
Async XLA Ops:
  0.6 22.5 %copy-start.9 = (s32[1,2048]{1,0:T(1,128)S(1)}, s32[1,2048]{1,0:T(1,128)}, u32[]{:S(2)}) copy-start(s32[1,2048]{1,0:T(1,128)} %param.14) | copy-start | bytes 24580
  0.6 22.5 %copy-start.4 = (f32[32,128,128]{2,1,0:T(8,128)S(1)}, f32[32,128,128]{2,1,0:T(8,128)}, u32[]{:S(2)}) copy-start(f32[32,128,128]{2,1,0:T(8,128)} %param.15) | copy-start | bytes 6291460
  0.7 13.5 %collective-permute-start.64 = (s32[1]{0:T(128)}, s32[1]{0:T(128)}, u32[]{:S(2)}, u32[]{:S(2)}) collective-permute-start(s32[1]{0:T(128)} %param.13), channel_id=1, source_target_pairs={{0,1},{1,0},{2,3},{3,2},{4,5},{5,4},{6,7},{7,6},{8,9},{9,8},{10,11... | collective-permute-start | bytes 20 | tf_op jit(solution)/shard_map/ppermute | solution.py:55
  14.8 7.8 %collective-permute-start.65 = (s32[1]{0:T(128)}, s32[1]{0:T(128)}, u32[]{:S(2)}, u32[]{:S(2)}) collective-permute-start(s32[1]{0:T(128)} %select_n.53), channel_id=1, source_target_pairs={{0,2},{1,3},{2,0},{3,1},{4,6},{5,7},{6,4},{7,5},{8,10},{9,11},{10,... | collective-permute-start | bytes 20 | tf_op jit(solution)/shard_map/ppermute | solution.py:55
  29.3 3.2 copy-start.1
  32.5 32.1 %collective-permute-start.16 = (bf16[1024,8,128]{2,1,0:T(8,128)(2,1)}, bf16[1024,8,128]{2,1,0:T(8,128)(2,1)}, u32[]{:S(2)}, u32[]{:S(2)}) collective-permute-start(bf16[1024,8,128]{2,1,0:T(8,128)(2,1)} %constant_dynamic-slice_fusion.3), channel_id=1, source_target_pairs={{0,1},{1,0},{2,3},{3,2},{4,5},{5,4},{6,7},{7,6},{8,9},{9,8},{10,11... | collective-permute-start | bytes 6291464 | tf_op jit(solution)/shard_map/cond/branch_1_fun/ppermute | solution.py:55
  34.6 6.1 %collective-permute-start.23 = (bf16[896,8,128]{2,1,0:T(8,128)(2,1)}, bf16[896,8,128]{2,1,0:T(8,128)(2,1)}, u32[]{:S(2)}, u32[]{:S(2)}) collective-permute-start(bf16[896,8,128]{2,1,0:T(8,128)(2,1)} %get-tuple-element.203), channel_id=1, source_target_pairs={{0,1},{1,2},{2,3},{4,5},{5,6},{6,7},{8,9},{9,10},{10,11},{12,13},{... | collective-permute-start | bytes 5505032 | tf_op jit(solution)/shard_map/cond/branch_1_fun/ppermute | solution.py:304
  38.3 6.0 %collective-permute-start.24 = (bf16[896,8,128]{2,1,0:T(8,128)(2,1)}, bf16[896,8,128]{2,1,0:T(8,128)(2,1)}, u32[]{:S(2)}, u32[]{:S(2)}) collective-permute-start(bf16[896,8,128]{2,1,0:T(8,128)(2,1)} %get-tuple-element.202), channel_id=1, source_target_pairs={{1,0},{2,1},{3,2},{5,4},{6,5},{7,6},{9,8},{10,9},{11,10},{13,12},{... | collective-permute-start | bytes 5505032 | tf_op jit(solution)/shard_map/cond/branch_1_fun/ppermute | solution.py:307
  70.8 68.9 %all-to-all-start.4 = ((bf16[1536,8,128]{2,1,0:T(8,128)(2,1)}), bf16[1536,8,128]{2,1,0:T(8,128)(2,1)S(1)}, u32[]{:S(2)}, u32[]{:S(2)}) async-start(bf16[1536,8,128]{2,1,0:T(8,128)(2,1)} %slice.50), calls=%async_computation.4 | async-start | bytes 6291456 | tf_op jit(solution)/shard_map/cond/branch_1_fun/all_to_all | solution.py:292
  78.3 25.4 %collective-permute-start.25 = (bf16[1024,8,128]{2,1,0:T(8,128)(2,1)S(1)}, bf16[1024,8,128]{2,1,0:T(8,128)(2,1)S(1)}, u32[]{:S(2)}, u32[]{:S(2)}) collective-permute-start(bf16[1024,8,128]{2,1,0:T(8,128)(2,1)S(1)} %constant_dynamic-slice_fusion.2), channel_id=1, source_target_pairs={{0,1},{1,0},{2,3},{3,2},{4,5},{5,4},{6,7},{7,6},{8,9},{9,8},{10,11... | collective-permute-start | bytes 6291464 | tf_op jit(solution)/shard_map/cond/branch_1_fun/ppermute | solution.py:55
  139.7 76.4 %copy-start.5 = (bf16[1536,8,128]{2,1,0:T(8,128)(2,1)}, bf16[1536,8,128]{2,1,0:T(8,128)(2,1)S(1)}, u32[]{:S(2)}) copy-start(bf16[1536,8,128]{2,1,0:T(8,128)(2,1)S(1)} %all-to-all-done.4) | copy-start | bytes 9437188 | tf_op jit(solution)/shard_map/cond
  139.7 80.0 %all-to-all-start.6 = ((bf16[1536,8,128]{2,1,0:T(8,128)(2,1)}), bf16[1536,8,128]{2,1,0:T(8,128)(2,1)}, u32[]{:S(2)}, u32[]{:S(2)}) async-start(bf16[1536,8,128]{2,1,0:T(8,128)(2,1)} %slice.51), calls=%async_computation.6 | async-start | bytes 6291456 | tf_op jit(solution)/shard_map/cond/branch_1_fun/all_to_all | solution.py:292
  145.3 14.0 %collective-permute-start.17 = (f32[64,64]{1,0:T(8,128)S(1)}, f32[64,64]{1,0:T(8,128)S(1)}, u32[]{:S(2)}, u32[]{:S(2)}) collective-permute-start(f32[64,64]{1,0:T(8,128)S(1)} %fusion.59), channel_id=1, source_target_pairs={{0,1},{1,0},{2,3},{3,2},{4,5},{5,4},{6,7},{7,6},{8,9},{9,8},{10,11... | collective-permute-start | bytes 49160 | tf_op jit(solution)/shard_map/cond/branch_1_fun/ppermute | solution.py:55
  159.3 34.7 %collective-permute-start.18 = (f32[64,64]{1,0:T(8,128)S(1)}, f32[64,64]{1,0:T(8,128)S(1)}, u32[]{:S(2)}, u32[]{:S(2)}) collective-permute-start(f32[64,64]{1,0:T(8,128)S(1)} %add.170), channel_id=1, source_target_pairs={{0,2},{1,3},{2,0},{3,1},{4,6},{5,7},{6,4},{7,5},{8,10},{9,11},{10,... | collective-permute-start | bytes 49160 | tf_op jit(solution)/shard_map/cond/branch_1_fun/ppermute | solution.py:55
  194.0 4.1 collective-permute-start.19
  198.1 4.3 collective-permute-start.20
  202.3 9.3 %collective-permute-start.21 = (f32[64,64]{1,0:T(8,128)S(1)}, f32[64,64]{1,0:T(8,128)S(1)}, u32[]{:S(2)}, u32[]{:S(2)}) collective-permute-start(f32[64,64]{1,0:T(8,128)S(1)} %add.173), channel_id=1, source_target_pairs={{0,16},{4,20},{8,24},{12,28},{16,0},{20,4},{24,8},{28,12},{1,17},{... | collective-permute-start | bytes 49160 | tf_op jit(solution)/shard_map/cond/branch_1_fun/ppermute | solution.py:55
  219.7 75.4 %all-to-all-start.5 = ((bf16[1536,8,128]{2,1,0:T(8,128)(2,1)}), bf16[1536,8,128]{2,1,0:T(8,128)(2,1)S(1)}, u32[]{:S(2)}, u32[]{:S(2)}) async-start(bf16[1536,8,128]{2,1,0:T(8,128)(2,1)} %bitcast.352), calls=%async_computation.5 | async-start | bytes 6291456 | tf_op jit(solution)/shard_map/cond/branch_1_fun/all_to_all | solution.py:297
  295.1 79.3 %all-to-all-start.7 = ((bf16[1536,8,128]{2,1,0:T(8,128)(2,1)}), bf16[1536,8,128]{2,1,0:T(8,128)(2,1)}, u32[]{:S(2)}, u32[]{:S(2)}) async-start(bf16[1536,8,128]{2,1,0:T(8,128)(2,1)} %bitcast.351), calls=%async_computation.7 | async-start | bytes 6291456 | tf_op jit(solution)/shard_map/cond/branch_1_fun/all_to_all | solution.py:297
  306.9 115.0 %collective-permute-start.22 = (bf16[1024,8,128]{2,1,0:T(8,128)(2,1)}, bf16[1024,8,128]{2,1,0:T(8,128)(2,1)}, u32[]{:S(2)}, u32[]{:S(2)}) collective-permute-start(bf16[1024,8,128]{2,1,0:T(8,128)(2,1)} %pad_dynamic-slice_fusion.3), channel_id=1, source_target_pairs={{0,1},{1,0},{2,3},{3,2},{4,5},{5,4},{6,7},{7,6},{8,9},{9,8},{10,11... | collective-permute-start | bytes 6291464 | tf_op jit(solution)/shard_map/cond/branch_1_fun/ppermute | solution.py:55
  374.3 3.8 copy-start.6
  378.0 54.4 %collective-permute-start.26 = (bf16[1024,8,128]{2,1,0:T(8,128)(2,1)}, bf16[1024,8,128]{2,1,0:T(8,128)(2,1)}, u32[]{:S(2)}, u32[]{:S(2)}) collective-permute-start(bf16[1024,8,128]{2,1,0:T(8,128)(2,1)} %pad_dynamic-slice_fusion.2), channel_id=1, source_target_pairs={{0,1},{1,0},{2,3},{3,2},{4,5},{5,4},{6,7},{7,6},{8,9},{9,8},{10,11... | collective-permute-start | bytes 6291464 | tf_op jit(solution)/shard_map/cond/branch_1_fun/ppermute | solution.py:55
  381.3 1.4 collective-permute-start.27
  382.7 7.2 %collective-permute-start.28 = (f32[64,64]{1,0:T(8,128)S(1)}, f32[64,64]{1,0:T(8,128)S(1)}, u32[]{:S(2)}, u32[]{:S(2)}) collective-permute-start(f32[64,64]{1,0:T(8,128)S(1)} %add.176), channel_id=1, source_target_pairs={{0,2},{1,3},{2,0},{3,1},{4,6},{5,7},{6,4},{7,5},{8,10},{9,11},{10,... | collective-permute-start | bytes 49160 | tf_op jit(solution)/shard_map/cond/branch_1_fun/ppermute | solution.py:55
  389.9 3.9 collective-permute-start.29
  393.8 3.9 collective-permute-start.30
  397.7 4.8 %collective-permute-start.31 = (f32[64,64]{1,0:T(8,128)S(1)}, f32[64,64]{1,0:T(8,128)S(1)}, u32[]{:S(2)}, u32[]{:S(2)}) collective-permute-start(f32[64,64]{1,0:T(8,128)S(1)} %add.179), channel_id=1, source_target_pairs={{0,16},{4,20},{8,24},{12,28},{16,0},{20,4},{24,8},{28,12},{1,17},{... | collective-permute-start | bytes 49160 | tf_op jit(solution)/shard_map/cond/branch_1_fun/ppermute | solution.py:55
